TPU v7x, 512 devices: a whole 4x8x8 slice. The times are simulated.
512 devices in a mesh: dp: 32 (over z, x), fsdp: 16 (over y, core).
Axes of the slice: x: 4, y: 8, z: 8, core: 2. Of those that a mesh axis runs over, the one named last changes fastest.
Arguments:
- momentum: float32 [32, 2, 1048576], P('dp', None, 'fsdp'), may hold values from -6 to 6
- gradients: bfloat16 [32, 2, 1048576], P('dp', None, 'fsdp'), may hold values from -6 to 6
- weight: bfloat16 [2, 1048576], P(None, 'fsdp'), may hold values from -2 to 2
- indices: int32 [32, 2, 4, 16384], P('dp', None, None, 'fsdp'), may hold values from 0 to 63, as said below
Outputs:
- moment_out: float32 [32, 2, 1048576], P('dp', None, 'fsdp')
- weight_out: bfloat16 [2, 1048576], replicated
Inputs may be any that keep to these rules, and one draw needn't show every extreme that they name: `indices`: for every replica, tensor and block the 4 components differ.
All inputs are finite; a program needn't handle non-finite values.
Results may differ from a plain program's by a relative error of at most 0.001.
Values may be sent and summed in bfloat16 or wider, within the bound.
A program may use at most 64 MiB of HBM per device.

v0:
```python
import math

import jax
import jax.numpy as jnp
from jax import lax
from jax.sharding import PartitionSpec as P

STRETCH = 64


decay_rate = 0.999
rate_step = 0.125


def pair_table():
    rows_k = jnp.arange(STRETCH, dtype=jnp.float32)[:, None]
    cols_n = jnp.arange(STRETCH, dtype=jnp.float32)[None, :]
    weights_k = jnp.where(rows_k == 0, math.sqrt(1.0 / STRETCH), math.sqrt(2.0 / STRETCH))
    cosine = weights_k * jnp.cos(math.pi * (2.0 * cols_n + 1.0) * rows_k / (2.0 * STRETCH))
    return jnp.kron(jnp.eye(2, dtype=jnp.float32), cosine)


def positions(own_lists):
    dims_in = own_lists.shape
    grouped = own_lists.reshape(dims_in[:-1] + (dims_in[-1] // 2, 2))
    grouped = grouped + STRETCH * jnp.arange(2, dtype=jnp.int32)
    grouped = jnp.swapaxes(grouped, -1, -2)
    return grouped.reshape(dims_in[:-2] + (2 * dims_in[-2], dims_in[-1] // 2))


def pick_values(spectrum, places):
    components = jnp.arange(2 * STRETCH, dtype=jnp.float32)
    picked = []
    for slot_index in range(places.shape[1]):
        matches = places[:, slot_index, :, None] == components
        picked.append(jnp.sum(jnp.where(matches, spectrum, 0.0), axis=-1))
    return jnp.stack(picked, axis=1)


def densify(values, places):
    components = jnp.arange(2 * STRETCH, dtype=jnp.float32)
    layer_count, slot_count, pair_count = places.shape
    dense_block = jnp.zeros((layer_count, pair_count, 2 * STRETCH), jnp.float32)
    for slot_index in range(slot_count):
        matches = places[:, slot_index, :, None] == components
        dense_block = dense_block + jnp.where(matches, values[:, slot_index, :, None], 0.0)
    return dense_block


def sum_replicas(running, values, places):

    def add_one(which, accum):
        one_values = lax.dynamic_index_in_dim(values, which, 0, keepdims=False)
        one_places = lax.dynamic_index_in_dim(places, which, 0, keepdims=False)
        return accum + densify(one_values, one_places)

    return lax.fori_loop(0, values.shape[0], add_one, running)


def apply_update(own_slice, summed, cosines):
    restored = jnp.einsum("lpk,kn->lpn", summed, cosines, precision=lax.Precision.HIGHEST)
    restored = restored.reshape(own_slice.shape)
    return (own_slice.astype(jnp.float32) - rate_step * restored).astype(jnp.bfloat16)


def shards(momentum, gradients, weight, indices):
    cosines = pair_table()
    layer_count, entries = weight.shape
    pair_count = entries // (2 * STRETCH)
    driven = decay_rate * momentum[0] + gradients[0].astype(jnp.float32)
    spectrum = jnp.einsum(
        "lpn,kn->lpk",
        driven.reshape(layer_count, pair_count, 2 * STRETCH),
        cosines,
        precision=lax.Precision.HIGHEST,
    )
    places = positions(indices[0]).astype(jnp.float32)
    chosen = pick_values(spectrum, places)
    own_dense = densify(chosen, places)
    own_back = jnp.einsum("lpk,kn->lpn", own_dense, cosines, precision=lax.Precision.HIGHEST)
    moment_out = (driven - own_back.reshape(layer_count, entries))[None]
    empty = jnp.zeros((layer_count, pair_count, 2 * STRETCH), jnp.float32)
    summed = sum_replicas(
        empty,
        lax.all_gather(chosen[None], "dp", axis=0, tiled=True),
        lax.all_gather(places[None], "dp", axis=0, tiled=True),
    )
    updated = apply_update(weight, summed, cosines)
    weight_out = lax.all_gather(updated, "fsdp", axis=1, tiled=True)
    return (moment_out, weight_out)


def solution(mesh):
    return jax.shard_map(
        shards,
        mesh=mesh,
        in_specs=(
            P("dp", None, "fsdp"),
            P("dp", None, "fsdp"),
            P(None, "fsdp"),
            P("dp", None, None, "fsdp"),
        ),
        out_specs=(P("dp", None, "fsdp"), P()),
        check_vma=False,
    )
```

profile of v0, /device:TPU:1, one launch (start us, length us, event | category | flops | bytes accessed | tf_op | source)
XLA Modules:
  0.0 346.1 jit_solution(1452210299479075758)
XLA Ops:
  14.4 80.6 %all-gather.5.cloned.1.call-done = f32[32,2,8,512]{3,2,1,0:T(8,128)} async-done(((f32[1,2,8,512]{3,2,1,0:T(8,128)}), f32[32,2,8,512]{3,2,1,0:T(8,128)}) %all-gather.5.cloned.1.call-update) | async-done | bytes 1048592 | tf_op jit(solution)/shard_map/all_gather | solution.py:86
  95.1 83.3 %all-gather.9.cloned.1.call-done = f32[64,8,512]{2,1,0:T(8,128)} async-done(((f32[2,8,512]{2,1,0:T(8,128)}), f32[64,8,512]{2,1,0:T(8,128)}) %all-gather.9.cloned.1.call-update) | async-done | bytes 1048592 | tf_op jit(solution)/shard_map/all_gather | solution.py:85
  178.4 104.8 %while.14 = (s32[]{:T(128)}, f32[2,512,128]{2,1,0:T(8,128)S(1)}, f32[32,2,8,512]{3,2,1,0:T(8,128)}, f32[32,2,8,512]{3,2,1,0:T(8,128)}, s32[]{:T(128)}, /*index=5*/s32[]{:T(128)}) while((s32[]{:T(128)}, f32[2,512,128]{2,1,0:T(8,128)S(1)}, f32[32,2,8,512]{3,2,1,0:T(8,128)}, f32[32,2,8,512]{3,2,1,0:T(8,128)}, s32[]{:T(128)}, ...), condition=%wide.region_9.10_spmd.clone, body=%wide.region_8.9_spmd.clone.sunk | while | flops 3276803 | bytes 1507419 | solution.py:57
  182.6 2.4 select_add_fusion.2
  185.8 2.4 select_add_fusion.2
  189.1 2.4 select_add_fusion.2
  192.4 2.4 select_add_fusion.2
  202.2 2.4 select_add_fusion.2
  205.5 2.4 select_add_fusion.2
  208.8 2.4 select_add_fusion.2
  212.0 2.4 select_add_fusion.2
  221.9 2.4 select_add_fusion.2
  225.1 2.4 select_add_fusion.2
  228.4 2.4 select_add_fusion.2
  231.7 2.4 select_add_fusion.2
  244.8 2.4 select_add_fusion.2
  248.1 2.4 select_add_fusion.2
  251.3 2.4 select_add_fusion.2
  254.6 2.4 select_add_fusion.2
  264.4 2.4 select_add_fusion.2
  267.7 2.4 select_add_fusion.2
  271.0 2.4 select_add_fusion.2
  286.3 45.6 %all-gather.7.cloned.1.call-done = bf16[2,1048576]{1,0:T(2,128)(2,1)} async-done(((bf16[2,65536]{1,0:T(2,128)(2,1)}), bf16[2,1048576]{1,0:T(2,128)(2,1)}) %all-gather.7.cloned.1.call-update) | async-done | bytes 4194320 | tf_op jit(solution)/shard_map/all_gather | solution.py:89
  331.9 7.7 %copy.50 = bf16[2,1048576]{1,0:T(2,128)(2,1)} copy(bf16[2,1048576]{1,0:T(2,128)(2,1)} %all-gather.7.cloned.1.call-done) | data formatting | bytes 8388608
  (213 shorter events, 68.3 us)
Async XLA Ops:
  7.2 3.3 copy-start.1
  7.2 3.3 copy-start
  7.2 87.9 %all-gather.5.cloned.1.call-start = ((), (), s32[]{:S(2)}) async-start(), calls=%async_computation | async-start | bytes 1081344 | tf_op jit(solution)/shard_map/all_gather | solution.py:86
  10.0 168.4 %all-gather.9.cloned.1.call-start = ((), (), s32[]{:S(2)}) async-start(), calls=%async_computation.2 | async-start | bytes 1081344 | tf_op jit(solution)/shard_map/all_gather | solution.py:85
  12.7 319.2 %all-gather.7.cloned.1.call-start = ((), (), s32[]{:S(2)}) async-start(), calls=%async_computation.1 | async-start | bytes 4456448 | tf_op jit(solution)/shard_map/all_gather | solution.py:89
  178.4 105.4 %copy-start.2 = (bf16[2,65536]{1,0:T(2,128)(2,1)S(1)}, bf16[2,65536]{1,0:T(2,128)(2,1)}, u32[]{:S(2)}) copy-start(bf16[2,65536]{1,0:T(2,128)(2,1)} %param.8) | copy-start | bytes 786436
Sparse Core Ops, SparseCore 0:
  11.8 83.2 all-gather.4
  98.8 79.5 all-gather.8
  285.2 46.6 all-gather.6
where the time goes:
time: 349 us; the launch traced here: 346 us
  waiting for transfers between devices  210 us (60%)
  other arithmetic  79.4 us (23%)
  local copies, waits for them, and re-layouts  38.5 us (11%)
  between operations  13.9 us (4%)
    all_gather x1, waiting for transfers between devices, shards(): lax.all_gather(chosen[None], 'dp', axis=0, tiled=True)  83.3 us
    all_gather x1, waiting for transfers between devices, shards(): lax.all_gather(places[None], 'dp', axis=0, tiled=True)  80.6 us
    add x32, other arithmetic, add_one(): return accum + densify(one_values, one_places)  75.9 us
    all_gather x1, waiting for transfers between devices, shards(): weight_out = lax.all_gather(updated, 'fsdp', axis=1, tiled=True)  45.6 us
    dynamic_slice x64, local copies, waits for them, and re-layouts, add_one(): one_values = lax.dynamic_index_in_dim(values, which, 0, keepdims=False)  26 us
    unnamed x8, local copies, waits for them, and re-layouts  8.89 us
  transfers between devices with their start and end apart: 3, of which 3 were waited for; matrix products, arithmetic and copies ran while one was open for 2% of the time, Pallas kernels for 0%

commit v1 on v0

v1 whole, which is shorter than its diff:
```python
import math

import jax
import jax.numpy as jnp
import numpy as np
from jax import lax
from jax.experimental import pallas as pl
from jax.experimental.pallas import tpu as pltpu
from jax.sharding import PartitionSpec as P

STRETCH = 64
TOPK = 4
NX, NY, NZ = 4, 8, 8
COLOURS = 8
ROWS = 128

decay_rate = 0.999
rate_step = 0.125

ALIKE = ((1, 1, -1), (-1, -1, 1), (-1, 2, 0), (1, -2, 0), (0, 3, -1), (0, -3, 1), (2, 4, 0))
AROUND = ((1, 0, 0), (-1, 0, 0), (0, 1, 0), (0, -1, 0), (0, 0, 1), (0, 0, -1))
ACROSS = ((0, 1, 1), (0, -1, -1)) + 6 * ((2, 0, 0),)


def pair_table():
    k = np.arange(STRETCH, dtype=np.float64)[:, None]
    n = np.arange(STRETCH, dtype=np.float64)[None, :]
    scale = np.where(k == 0, math.sqrt(1.0 / STRETCH), math.sqrt(2.0 / STRETCH))
    cosine = scale * np.cos(math.pi * (2.0 * n + 1.0) * k / (2.0 * STRETCH))
    return np.kron(np.eye(2), cosine).astype(np.float32)


def iota(shape, dim):
    return lax.broadcasted_iota(jnp.int32, shape, dim)


def exact_dot(a, b):
    return jnp.dot(a, b, precision=lax.Precision.HIGHEST, preferred_element_type=jnp.float32)


def lane_gather(values, lanes):
    return jnp.take_along_axis(values, lanes, axis=1, mode="promise_in_bounds")


def spread(packed, piece, slot):
    return lane_gather(packed, 8 * piece + 2 * slot + iota((8, 128), 1) // STRETCH)


def transform_kernel(momentum, gradients, indices, forward, backward, moment_out, message):
    lane = iota((8, 128), 1)
    row = iota((8, 128), 0)
    deep_row = iota((128, 128), 0)
    deep_lane = iota((128, 128), 1)

    packed = jnp.zeros((8 * COLOURS, 128), jnp.float32)
    mine = (lane // 2) % 4 == row // 2
    for slot in range(TOPK):
        tiles = []
        for share in range(COLOURS):
            columns = pl.ds(128 * share, 128)
            first = indices[pl.ds(slot, 1), columns]
            second = indices[pl.ds(TOPK + slot, 1), columns]
            both = jnp.where(row % 2 == 0, first, second)
            tiles.append(jnp.where(mine, both, 0).astype(jnp.float32))
        place = (deep_row // 8 == deep_lane // 8) & (deep_row % 2 == deep_lane % 2) & ((deep_lane // 2) % 4 == slot)
        packed = packed + jnp.dot(
            jnp.concatenate(tiles, axis=0).astype(jnp.bfloat16),
            jnp.where(place, 1.0, 0.0).astype(jnp.bfloat16),
            preferred_element_type=jnp.float32,
        )

    component = (lane % STRETCH).astype(jnp.float32)
    for share in range(COLOURS):
        rows = pl.ds(ROWS * share, ROWS)
        driven = decay_rate * momentum[rows, :] + gradients[rows, :].astype(jnp.float32)
        spectrum = exact_dot(driven, forward[...])
        places = packed[8 * share : 8 * share + 8]
        lanes = places.astype(jnp.int32) + STRETCH * (lane % 2)
        values = jnp.zeros((8, 128), jnp.float32)
        dense = []
        for piece in range(16):
            part = spectrum[8 * piece : 8 * piece + 8]
            values = jnp.where(lane // 8 == piece, lane_gather(part, lanes), values)
            kept = spread(places, piece, 0) == component
            for slot in range(1, TOPK):
                kept = kept | (spread(places, piece, slot) == component)
            dense.append(jnp.where(kept, part, 0.0))
        message[share, pl.ds(0, 8), :] = values
        message[share, pl.ds(8, 8), :] = places
        moment_out[rows, :] = driven - exact_dot(jnp.concatenate(dense, axis=0), backward[...])


def share_kernel(message, weight, backward, whole, inbox, total, list_sent, list_here, alike_sent, alike_here,
                 around_sent, around_here, twin_sent, twin_here):
    dp = lax.axis_index("dp")
    fsdp = lax.axis_index("fsdp")
    z, x = dp // NX, dp % NX
    y, core = fsdp // 2, fsdp % 2
    colour = (2 * x + y + 3 * z) % COLOURS

    def chip(dx, dy, dz):
        return (((z + dz + NZ) % NZ) * NX + (x + dx + NX) % NX, ((y + dy + NY) % NY) * 2 + core)

    twin = (dp, y * 2 + 1 - core)

    def plane_step(which):
        turn = which // NX
        dz = jnp.where(turn % 2 == 1, (turn + 1) // 2, (NZ - turn // 2) % NZ)
        return which % NX, dz

    barrier = pltpu.get_barrier_semaphore()

    def greet(which, carry):
        dx, dz = plane_step(which)
        pl.semaphore_signal(barrier, 1, device_id=chip(-dx, 0, -dz))
        return carry

    lax.fori_loop(1, NX * NZ, greet, 0)
    others = sorted(set(ALIKE + AROUND + ACROSS))
    for dx, dy, dz in others:
        pl.semaphore_signal(barrier, 1, device_id=chip(-dx, -dy, -dz))
    pl.semaphore_signal(barrier, 1, device_id=twin)
    pl.semaphore_wait(barrier, NX * NZ - 1 + len(others) + 1)

    def send_list(step, carry):
        which = NX * NZ - 1 - step
        dx, dz = plane_step(which)
        theirs = (colour + 2 * dx + 3 * dz) % COLOURS
        pltpu.make_async_remote_copy(
            src_ref=message.at[theirs], dst_ref=inbox.at[which], send_sem=list_sent,
            recv_sem=list_here.at[which], device_id=chip(dx, 0, dz),
        ).start()
        return carry

    lax.fori_loop(0, NX * NZ - 1, send_list, 0)

    lane = iota((8, 128), 1)
    component = (lane % STRETCH).astype(jnp.float32)

    def add_list(values, places, first):
        for piece in range(16):
            rows = pl.ds(8 * piece, 8)
            summed = jnp.zeros((8, 128), jnp.float32) if first else total[rows, :]
            for slot in range(TOPK):
                kept = spread(places, piece, slot) == component
                summed = summed + jnp.where(kept, spread(values, piece, slot), 0.0)
            total[rows, :] = summed

    add_list(message[colour, pl.ds(0, 8), :], message[colour, pl.ds(8, 8), :], True)

    def take_list(which, carry):
        pltpu.make_async_copy(inbox.at[which], inbox.at[which], list_here.at[which]).wait()
        add_list(inbox[which, pl.ds(0, 8), :], inbox[which, pl.ds(8, 8), :], False)
        return carry

    lax.fori_loop(1, NX * NZ, take_list, 0)

    restored = exact_dot(total[...], backward[...])
    own = weight[pl.ds(pl.multiple_of(colour * ROWS, ROWS), ROWS), :].astype(jnp.float32)
    whole[y, core, colour] = (own - rate_step * restored).astype(jnp.bfloat16)

    def block(plane, parity, tint):
        return whole.at[plane, parity, tint]

    def to_twin(plane, tint):
        pltpu.make_async_remote_copy(
            src_ref=block(plane, core, tint), dst_ref=block(plane, core, tint), send_sem=twin_sent,
            recv_sem=twin_here, device_id=twin,
        ).start()

    def pass_on(plane, number):
        for way, step in enumerate(AROUND + (ACROSS[number],)):
            pltpu.make_async_remote_copy(
                src_ref=block(plane, core, colour), dst_ref=block(plane, core, colour),
                send_sem=around_sent, recv_sem=around_here.at[way, number], device_id=chip(*step),
            ).start()
        to_twin(plane, colour)

    def await_block(plane, tint, semaphore):
        pltpu.make_async_copy(block(plane, core, tint), block(plane, core, tint), semaphore).wait()

    for number in reversed(range(len(ALIKE))):
        pltpu.make_async_remote_copy(
            src_ref=block(y, core, colour), dst_ref=block(y, core, colour), send_sem=alike_sent,
            recv_sem=alike_here.at[number], device_id=chip(*ALIKE[number]),
        ).start()
    pass_on(y, 0)
    for number, step in enumerate(ALIKE):
        plane = (y - step[1] + NY) % NY
        await_block(plane, colour, alike_here.at[number])
        pass_on(plane, number + 1)

    for number in range(NY):
        back = 0 if number == 0 else ALIKE[number - 1][1]
        for way, step in enumerate(AROUND + (ACROSS[number],)):
            plane = (y - step[1] - back + 2 * NY) % NY
            tint = (colour - 2 * step[0] - step[1] - 3 * step[2] + 2 * COLOURS) % COLOURS
            await_block(plane, tint, around_here.at[way, number])
            to_twin(plane, tint)

    def await_bytes(ref, semaphore):
        pltpu.make_async_copy(ref, ref, semaphore).wait()

    await_bytes(inbox.at[pl.ds(1, NX * NZ - 1)], list_sent)
    await_bytes(whole.at[pl.ds(0, 7), core, 0], alike_sent)
    await_bytes(whole.at[pl.ds(0, 7), core], around_sent)
    await_bytes(whole.at[:, core], twin_sent)
    await_bytes(whole.at[:, 1 - core], twin_here)


def as_rows(array):
    layers, entries = array.shape
    return array.reshape(layers, entries // 128, 128).transpose(1, 0, 2).reshape(layers * entries // 128, 128)


def from_rows(array, layers):
    pieces = array.shape[0] // layers
    return array.reshape(pieces, layers, 128).transpose(1, 0, 2).reshape(layers, pieces * 128)


def shards(momentum, gradients, weight, indices):
    layers, entries = weight.shape
    table = pair_table()
    forward, backward = jnp.asarray(table.T), jnp.asarray(table)
    in_vmem = pl.BlockSpec(memory_space=pltpu.VMEM)
    moment_rows, message = pl.pallas_call(
        transform_kernel,
        out_shape=(
            jax.ShapeDtypeStruct((layers * entries // 128, 128), jnp.float32),
            jax.ShapeDtypeStruct((COLOURS, 16, 128), jnp.float32),
        ),
        in_specs=[in_vmem] * 5,
        out_specs=(in_vmem, in_vmem),
        compiler_params=pltpu.CompilerParams(vmem_limit_bytes=24 * 2**20),
    )(as_rows(momentum[0]), as_rows(gradients[0]), indices.reshape(layers * TOPK, -1), forward, backward)
    dma = pltpu.SemaphoreType.DMA
    whole = pl.pallas_call(
        share_kernel,
        out_shape=jax.ShapeDtypeStruct((NY, 2, COLOURS, ROWS, 128), jnp.bfloat16),
        in_specs=[in_vmem] * 3,
        out_specs=in_vmem,
        scratch_shapes=[
            pltpu.VMEM((NX * NZ, 16, 128), jnp.float32),
            pltpu.VMEM((ROWS, 128), jnp.float32),
            dma, dma((NX * NZ,)), dma, dma((len(ALIKE),)), dma, dma((7, NY)), dma, dma,
        ],
        compiler_params=pltpu.CompilerParams(
            collective_id=0, has_side_effects=True, vmem_limit_bytes=24 * 2**20
        ),
    )(message, as_rows(weight), backward)
    weight_out = from_rows(whole.reshape(-1, 128), layers)
    return (from_rows(moment_rows, layers)[None], weight_out)


def solution(mesh):
    return jax.shard_map(
        shards,
        mesh=mesh,
        in_specs=(
            P("dp", None, "fsdp"),
            P("dp", None, "fsdp"),
            P(None, "fsdp"),
            P("dp", None, None, "fsdp"),
        ),
        out_specs=(P("dp", None, "fsdp"), P()),
        check_vma=False,
    )
```

time: 349 us -> 69.7 us (0.20)
  waiting for transfers between devices: 210 us -> 0 us
  other arithmetic: 79.4 us -> 0 us
  Pallas kernels: 0 us -> 60.4 us
  local copies, waits for them, and re-layouts: 38.5 us -> 8.24 us
  between operations: 13.9 us -> 0.65 us
    all_gather x3 -> x0, waiting for transfers between devices: 210 us -> none  [the longest x1 83.3 us: shards(): lax.all_gather(chosen[None], 'dp', axis=0, tiled=True)]
    add x32 -> x0, other arithmetic: 75.9 us -> none  [add_one(): return accum + densify(one_values, one_places)]
    pallas_call x0 -> x2, Pallas kernels: none -> 60.4 us  [the longest x1 57.5 us: shards(): pl.pallas_call(share_kernel, out_shape=jax.ShapeDtypeStruct((NY, 2, COLOU...]
    dynamic_slice x96 -> x0, local copies, waits for them, and re-layouts: 26.9 us -> none  [the longest x64 26 us: add_one(): one_values = lax.dynamic_index_in_dim(values, which, 0, keepdims=False)]
    unnamed x8 -> x13, local copies, waits for them, and re-layouts: 8.89 us -> 7.47 us
  transfers between devices with their start and end apart: 3 -> 0, of which waited for: 3 -> 0; matrix products, arithmetic and copies ran while one was open for 2% -> 0% of each run, Pallas kernels for 0% -> 0%
where the time goes in v1:
time: 69.7 us; the launch traced here: 69.3 us
  Pallas kernels  60.4 us (87%)
  local copies, waits for them, and re-layouts  8.24 us (12%)
    pallas_call x1, Pallas kernels, shards(): pl.pallas_call(share_kernel, out_shape=jax.ShapeDtypeStruct((NY, 2, COLOU...  57.5 us
    unnamed x13, local copies, waits for them, and re-layouts  7.47 us
    pallas_call x1, Pallas kernels, shards(): pl.pallas_call(transform_kernel, out_shape=(jax.ShapeDtypeStruct((layers...  2.91 us

profile of v1, /device:TPU:1, one launch (start us, length us, event | category | flops | bytes accessed | tf_op | source)
XLA Modules:
  0.0 69.3 jit_solution(6959986472147475247)
XLA Ops:
  0.6 0.8 %reshape.27.indices = s32[8,1024]{1,0:T(8,128)S(1)} reshape(s32[1,2,4,1024]{3,2,1,0:T(4,128)} %param.9) | data formatting | bytes 65536 | tf_op jit(solution)/shard_map/reshape | solution.py:235
  1.4 0.0 copy-start
  1.4 1.0 %copy-done = f32[1,2,65536]{2,1,0:T(2,128)S(1)} copy-done((f32[1,2,65536]{2,1,0:T(2,128)S(1)}, f32[1,2,65536]{2,1,0:T(2,128)}, u32[]{:S(2)}) %copy-start) | copy-done | bytes 524312
  2.4 0.0 copy-start.1
  2.5 0.8 %copy-done.1 = f32[128,128]{1,0:T(8,128)S(1)} copy-done((f32[128,128]{1,0:T(8,128)S(1)}, f32[128,128]{1,0:T(8,128)}, u32[]{:S(2)}) %copy-start.1) | copy-done | bytes 65560
  3.3 0.0 copy-start.4
  3.3 0.9 %copy-done.4 = bf16[1,2,65536]{2,1,0:T(2,128)(2,1)S(1)} copy-done((bf16[1,2,65536]{2,1,0:T(2,128)(2,1)S(1)}, bf16[1,2,65536]{2,1,0:T(2,128)(2,1)}, u32[]{:S(2)}) %copy-start.4) | copy-done | bytes 262168
  4.2 0.0 copy-start.5
  4.2 0.8 %copy-done.5 = f32[128,128]{1,0:T(8,128)S(1)} copy-done((f32[128,128]{1,0:T(8,128)S(1)}, f32[128,128]{1,0:T(8,128)}, u32[]{:S(2)}) %copy-start.5) | copy-done | bytes 65560
  5.1 2.9 %shard_map.77 = (f32[1024,128]{1,0:T(8,128)}, f32[8,16,128]{2,1,0:T(8,128)S(1)}) custom-call(f32[1024,128]{1,0:T(8,128)S(1)} %bitcast.26, bf16[1024,128]{1,0:T(8,128)(2,1)S(1)} %bitcast.28, s32[8,1024]{1,0:T(8,128)S(1)} %reshape.27.indices, f32[128,128]{1,0:T(8,128)S(1)} %copy-done.5, f32[128,128]{1,0:T(8,128)S(1)} %copy-done.1), custom_call_target="tpu_custom_call" | custom-call | tf_op jit(solution)/shard_map/pallas_call | solution.py:226
  8.0 0.0 copy-start.2
  8.0 0.8 %copy-done.2 = f32[128,128]{1,0:T(8,128)S(1)} copy-done((f32[128,128]{1,0:T(8,128)S(1)}, f32[128,128]{1,0:T(8,128)}, u32[]{:S(2)}) %copy-start.2) | copy-done | bytes 65560
  8.8 0.0 copy-start.3
  8.8 0.9 %copy-done.3 = bf16[2,65536]{1,0:T(2,128)(2,1)S(1)} copy-done((bf16[2,65536]{1,0:T(2,128)(2,1)S(1)}, bf16[2,65536]{1,0:T(2,128)(2,1)}, u32[]{:S(2)}) %copy-start.3) | copy-done | bytes 262168
  9.8 57.5 %shard_map.78 = bf16[8,2,8,128,128]{4,3,2,1,0:T(8,128)(2,1)S(1)} custom-call(f32[8,16,128]{2,1,0:T(8,128)S(1)} %get-tuple-element.5.message, bf16[1024,128]{1,0:T(8,128)(2,1)S(1)} %bitcast.27, f32[128,128]{1,0:T(8,128)S(1)} %copy-done.2), custom_call_target="tpu_custom_call" | custom-call | tf_op jit(solution)/shard_map/pallas_call | solution.py:237
  67.3 2.0 %copy.14 = bf16[2,1048576]{1,0:T(2,128)(2,1)} copy(bf16[2,1048576]{1,0:T(2,128)(2,1)S(1)} %bitcast.25) | data formatting | bytes 8388608
Async XLA Ops:
  1.4 1.0 %copy-start = (f32[1,2,65536]{2,1,0:T(2,128)S(1)}, f32[1,2,65536]{2,1,0:T(2,128)}, u32[]{:S(2)}) copy-start(f32[1,2,65536]{2,1,0:T(2,128)} %param.6) | copy-start | bytes 1572868
  2.4 0.8 %copy-start.1 = (f32[128,128]{1,0:T(8,128)S(1)}, f32[128,128]{1,0:T(8,128)}, u32[]{:S(2)}) copy-start(f32[128,128]{1,0:T(8,128)} %constant.5.clone.backward) | copy-start | bytes 196612
  3.3 0.9 %copy-start.4 = (bf16[1,2,65536]{2,1,0:T(2,128)(2,1)S(1)}, bf16[1,2,65536]{2,1,0:T(2,128)(2,1)}, u32[]{:S(2)}) copy-start(bf16[1,2,65536]{2,1,0:T(2,128)(2,1)} %param.7) | copy-start | bytes 786436
  4.2 0.8 %copy-start.5 = (f32[128,128]{1,0:T(8,128)S(1)}, f32[128,128]{1,0:T(8,128)}, u32[]{:S(2)}) copy-start(f32[128,128]{1,0:T(8,128)} %constant.4.clone.forward) | copy-start | bytes 196612
  8.0 0.8 %copy-start.2 = (f32[128,128]{1,0:T(8,128)S(1)}, f32[128,128]{1,0:T(8,128)}, u32[]{:S(2)}) copy-start(f32[128,128]{1,0:T(8,128)} %constant.5.clone.backward) | copy-start | bytes 196612
  8.8 0.9 %copy-start.3 = (bf16[2,65536]{1,0:T(2,128)(2,1)S(1)}, bf16[2,65536]{1,0:T(2,128)(2,1)}, u32[]{:S(2)}) copy-start(bf16[2,65536]{1,0:T(2,128)(2,1)} %param.8) | copy-start | bytes 786436

commit v2 on v1

v2 whole, which is shorter than its diff:
```python
import math

import jax
import jax.numpy as jnp
import numpy as np
from jax import lax
from jax.experimental import pallas as pl
from jax.experimental.pallas import tpu as pltpu
from jax.sharding import PartitionSpec as P

STRETCH = 64
TOPK = 4
NX, NY, NZ = 4, 8, 8
COLOURS = 8
ROWS = 128

decay_rate = 0.999
rate_step = 0.125

ALIKE = ((1, 1, -1), (-1, -1, 1), (-1, 2, 0), (1, -2, 0), (0, 3, -1), (0, -3, 1), (2, 4, 0))
AROUND = ((1, 0, 0), (-1, 0, 0), (0, 1, 0), (0, -1, 0), (0, 0, 1), (0, 0, -1))
ACROSS = ((0, 1, 1), (0, -1, -1)) + 6 * ((2, 0, 0),)


def pair_tables():
    k = np.arange(STRETCH, dtype=np.float64)[:, None]
    n = np.arange(STRETCH, dtype=np.float64)[None, :]
    scale = np.where(k == 0, math.sqrt(1.0 / STRETCH), math.sqrt(2.0 / STRETCH))
    cosine = np.kron(np.eye(2), scale * np.cos(math.pi * (2.0 * n + 1.0) * k / (2.0 * STRETCH)))

    return np.stack([cosine.T, cosine]).astype(np.float32)


def iota(shape, dim):
    return lax.broadcasted_iota(jnp.int32, shape, dim)


def lane_gather(values, lanes):
    return jnp.take_along_axis(values, lanes, axis=1, mode="promise_in_bounds")


def split(values):
    high = values.astype(jnp.bfloat16)
    low = (values - high.astype(jnp.float32)).astype(jnp.bfloat16)
    return jnp.concatenate([high, low], axis=1)


def table_dot(rows, table):
    both = jnp.dot(
        split(rows),
        jnp.concatenate([table, table], axis=0),
        preferred_element_type=jnp.float32,
    )
    return both[:, :128] + both[:, 128:]


def sync_kernel(momentum_in, gradients_in, weight_in, indices_in, tables_in, moment_out, whole,
                momentum, gradients, weight, indices, tables, kept_columns, message, inbox, loaded,
                list_sent, list_here, alike_sent, alike_here, around_sent, around_here, twin_sent, twin_here):
    dp = lax.axis_index("dp")
    fsdp = lax.axis_index("fsdp")
    z, x = lax.div(dp, NX), lax.rem(dp, NX)
    y, core = lax.div(fsdp, 2), lax.rem(fsdp, 2)
    colour = lax.rem(2 * x + y + 3 * z, COLOURS)
    xs = [lax.rem(x + d, NX) for d in range(NX)]
    ys = [lax.rem(y + d, NY) for d in range(NY)]
    zs = [lax.rem(z + d, NZ) for d in range(NZ)]
    tints = [lax.rem(colour + d, COLOURS) for d in range(COLOURS)]

    def chip(dx, dy, dz):
        return (zs[dz % NZ] * NX + xs[dx % NX], ys[dy % NY] * 2 + core)

    twin = (dp, y * 2 + 1 - core)

    own_rows = pl.ds(pl.multiple_of(colour * ROWS, ROWS), ROWS)
    loads = [
        pltpu.make_async_copy(source, target, loaded.at[number])
        for number, (source, target) in enumerate((
            (indices_in, indices), (tables_in, tables), (momentum_in, momentum),
            (gradients_in, gradients), (weight_in.at[own_rows], weight),
        ))
    ]
    for load in loads:
        load.start()

    plane = [(dx, dz) for dz in (4, 3, 5, 2, 6, 1, 7, 0) for dx in (2, 1, 3, 0) if (dx, dz) != (0, 0)]
    barrier = pltpu.get_barrier_semaphore()
    for dx, dz in plane:
        pl.semaphore_signal(barrier, 1, device_id=chip(dx, 0, dz))
    others = sorted(set(ALIKE + AROUND + ACROSS) - {(dx, 0, dz) for dx, dy, dz in AROUND if dy == 0} - {(2, 0, 0)})
    for dx, dy, dz in others:
        pl.semaphore_signal(barrier, 1, device_id=chip(-dx, -dy, -dz))
    pl.semaphore_signal(barrier, 1, device_id=twin)

    lane = iota((8, 128), 1)
    even = iota((TOPK, 128), 1) % 2 == 0
    component = iota((STRETCH, 128), 0)

    for load in loads[:4]:
        load.wait()

    forward, backward = split(tables[0]), split(tables[1])

    def driven_rows(rows):
        return decay_rate * momentum[rows, :] + gradients[rows, :].astype(jnp.float32)

    def transform(share, carry):
        rows = pl.ds(pl.multiple_of(share * ROWS, ROWS), ROWS)
        columns = table_dot(driven_rows(rows), forward).T
        listed = jnp.concatenate([indices[0, :, rows], indices[1, :, rows]], axis=0)
        below = lane_gather(listed, (lane + 127) % 128)
        above = lane_gather(listed, (lane + 1) % 128)
        places = (
            jnp.where(even, listed[:TOPK], below[TOPK:]),
            jnp.where(even, above[:TOPK], listed[TOPK:]),
        )
        for half in range(2):
            part = columns[STRETCH * half : STRETCH * (half + 1)]
            kept = jnp.zeros((STRETCH, 128), jnp.float32)
            for slot in range(TOPK):
                match = component == places[half][slot : slot + 1]
                picked = jnp.where(match, part, 0.0)
                message[share, half, pl.ds(slot, 1), :] = jnp.sum(picked, axis=0, keepdims=True)
                kept = jnp.where(match, part, kept)
            kept_columns[share, pl.ds(STRETCH * half, STRETCH), :] = kept
        message[share, 2] = (places[0] + 65536 * places[1]).astype(jnp.float32)
        return carry

    lax.fori_loop(0, COLOURS, transform, 0)

    pl.semaphore_wait(barrier, len(plane) + len(others) + 1)

    for number, (dx, dz) in enumerate(plane):
        pltpu.make_async_remote_copy(
            src_ref=message.at[tints[(2 * dx + 3 * dz) % COLOURS]], dst_ref=inbox.at[number], send_sem=list_sent,
            recv_sem=list_here.at[number], device_id=chip(dx, 0, dz),
        ).start()

    def keep_rest(share, carry):
        rows = pl.ds(pl.multiple_of(share * ROWS, ROWS), ROWS)
        moment_out[rows, :] = driven_rows(rows) - table_dot(kept_columns[share].T, backward)
        return carry

    lax.fori_loop(0, COLOURS, keep_rest, 0)

    def add_list(number, summed):
        pltpu.make_async_copy(inbox.at[number], inbox.at[number], list_here.at[number]).wait()
        coded = inbox[number, 2].astype(jnp.int32)
        places = (coded % 65536, coded // 65536)
        halves = []
        for half in range(2):
            term = jnp.zeros((STRETCH, 128), jnp.float32)
            for slot in range(TOPK):
                match = component == places[half][slot : slot + 1]
                term = jnp.where(match, inbox[number, half, pl.ds(slot, 1), :], term)
            halves.append(summed[STRETCH * half : STRETCH * (half + 1)] + term)
        return jnp.concatenate(halves, axis=0)

    summed = lax.fori_loop(0, len(plane), add_list, kept_columns[colour])
    restored = table_dot(summed.T, backward)
    loads[4].wait()
    whole[y, core, colour] = (weight[...].astype(jnp.float32) - rate_step * restored).astype(jnp.bfloat16)

    def block(plane, tint):
        return whole.at[plane, core, tint]

    def to_twin(plane, tint):
        pltpu.make_async_remote_copy(
            src_ref=block(plane, tint), dst_ref=block(plane, tint), send_sem=twin_sent,
            recv_sem=twin_here, device_id=twin,
        ).start()

    def pass_on(plane, number):
        for way, step in enumerate(AROUND + (ACROSS[number],)):
            pltpu.make_async_remote_copy(
                src_ref=block(plane, colour), dst_ref=block(plane, colour),
                send_sem=around_sent, recv_sem=around_here.at[way, number], device_id=chip(*step),
            ).start()
        to_twin(plane, colour)

    def await_block(plane, tint, semaphore):
        pltpu.make_async_copy(block(plane, tint), block(plane, tint), semaphore).wait()

    for number in reversed(range(len(ALIKE))):
        pltpu.make_async_remote_copy(
            src_ref=block(y, colour), dst_ref=block(y, colour), send_sem=alike_sent,
            recv_sem=alike_here.at[number], device_id=chip(*ALIKE[number]),
        ).start()
    pass_on(y, 0)
    for number, step in enumerate(ALIKE):
        there = ys[-step[1] % NY]
        await_block(there, colour, alike_here.at[number])
        pass_on(there, number + 1)

    for number in range(NY):
        back = 0 if number == 0 else ALIKE[number - 1][1]
        for way, step in enumerate(AROUND + (ACROSS[number],)):
            there = ys[(-step[1] - back) % NY]
            tint = tints[-(2 * step[0] + step[1] + 3 * step[2]) % COLOURS]
            await_block(there, tint, around_here.at[way, number])
            to_twin(there, tint)

    def await_bytes(ref, semaphore):
        pltpu.make_async_copy(ref, ref, semaphore).wait()

    await_bytes(inbox, list_sent)
    await_bytes(whole.at[pl.ds(0, 7), core, 0], alike_sent)
    await_bytes(whole.at[pl.ds(0, 7), core], around_sent)
    await_bytes(whole.at[:, core], twin_sent)
    await_bytes(whole.at[:, 1 - core], twin_here)


def as_rows(array):
    layers, entries = array.shape
    return array.reshape(layers, entries // 128, 128).transpose(1, 0, 2).reshape(layers * entries // 128, 128)


def from_rows(array, layers):
    pieces = array.shape[0] // layers
    return array.reshape(pieces, layers, 128).transpose(1, 0, 2).reshape(layers, pieces * 128)


def shards(momentum, gradients, weight, indices):
    layers, entries = weight.shape
    rows = layers * entries // 128
    in_hbm = pl.BlockSpec(memory_space=pltpu.HBM)
    in_vmem = pl.BlockSpec(memory_space=pltpu.VMEM)
    dma = pltpu.SemaphoreType.DMA
    peers = NX * NZ - 1
    operands = (
        as_rows(momentum[0]), as_rows(gradients[0]), as_rows(weight), indices[0], jnp.asarray(pair_tables())
    )
    moment_rows, whole = pl.pallas_call(
        sync_kernel,
        out_shape=(
            jax.ShapeDtypeStruct((rows, 128), jnp.float32),
            jax.ShapeDtypeStruct((NY, 2, COLOURS, ROWS, 128), jnp.bfloat16),
        ),
        in_specs=[in_hbm] * 5,
        out_specs=(in_vmem, in_vmem),
        scratch_shapes=[
            pltpu.VMEM((rows, 128), jnp.float32),
            pltpu.VMEM((rows, 128), jnp.bfloat16),
            pltpu.VMEM((ROWS, 128), jnp.bfloat16),
            pltpu.VMEM(indices.shape[1:], jnp.int32),
            pltpu.VMEM((2, 128, 128), jnp.float32),
            pltpu.VMEM((COLOURS, 128, ROWS), jnp.float32),
            pltpu.VMEM((COLOURS, 3, TOPK, 128), jnp.float32),
            pltpu.VMEM((peers, 3, TOPK, 128), jnp.float32),
            dma((5,)), dma, dma((peers,)), dma, dma((len(ALIKE),)), dma, dma((7, NY)), dma, dma,
        ],
        compiler_params=pltpu.CompilerParams(
            collective_id=0, has_side_effects=True, vmem_limit_bytes=24 * 2**20
        ),
    )(*(pltpu.with_memory_space_constraint(operand, pltpu.HBM) for operand in operands))
    weight_out = from_rows(whole.reshape(-1, 128), layers)
    return (from_rows(moment_rows, layers)[None], weight_out)


def solution(mesh):
    return jax.shard_map(
        shards,
        mesh=mesh,
        in_specs=(
            P("dp", None, "fsdp"),
            P("dp", None, "fsdp"),
            P(None, "fsdp"),
            P("dp", None, None, "fsdp"),
        ),
        out_specs=(P("dp", None, "fsdp"), P()),
        check_vma=False,
    )
```

time: 69.7 us -> 49.6 us (0.71)
  Pallas kernels: 60.4 us -> 46 us
  local copies, waits for them, and re-layouts: 8.24 us -> 2.81 us
    pallas_call x2 -> x1, Pallas kernels: 60.4 us -> 46 us  [shards(): pl.pallas_call(sync_kernel, out_shape=(jax.ShapeDtypeStruct((rows, 128),...]
    unnamed x13 -> x2, local copies, waits for them, and re-layouts: 7.47 us -> 2.81 us
    reshape x1 -> x0, local copies, waits for them, and re-layouts: 0.77 us -> none  [shards(): indices.reshape(layers * TOPK, -1)]
where the time goes in v2:
time: 49.6 us; the launch traced here: 49.4 us
  Pallas kernels  46 us (93%)
  local copies, waits for them, and re-layouts  2.81 us (6%)
  between operations  0.64 us (1%)
    pallas_call x1, Pallas kernels, shards(): pl.pallas_call(sync_kernel, out_shape=(jax.ShapeDtypeStruct((rows, 128),...  46 us
    unnamed x2, local copies, waits for them, and re-layouts  2.81 us

profile of v2, /device:TPU:1, one launch (start us, length us, event | category | flops | bytes accessed | tf_op | source)
XLA Modules:
  0.0 49.4 jit_solution(8484693985592327465)
XLA Ops:
  0.6 46.0 %shard_map.68 = (f32[1024,128]{1,0:T(8,128)S(1)}, bf16[8,2,8,128,128]{4,3,2,1,0:T(8,128)(2,1)S(1)}) custom-call(f32[1024,128]{1,0:T(8,128)} %bitcast.28, bf16[1024,128]{1,0:T(8,128)(2,1)} %bitcast.29, bf16[1024,128]{1,0:T(8,128)(2,1)} %bitcast.30, s32[2,4,1024]{2,1,0:T(4,128)} %bitcast.31, f32[2,128,128]{2,1,0:T(8,128)} %constant.2.clone.tables_in), custom_call_target="tpu_custom_call" | custom-call | tf_op jit(solution)/shard_map/pallas_call | solution.py:233
  46.6 0.8 %copy.14 = f32[1,2,65536]{2,1,0:T(2,128)} copy(f32[1,2,65536]{2,1,0:T(2,128)S(1)} %bitcast.27) | data formatting | bytes 1048576
  47.4 2.0 %copy.15 = bf16[2,1048576]{1,0:T(2,128)(2,1)} copy(bf16[2,1048576]{1,0:T(2,128)(2,1)S(1)} %bitcast.26) | data formatting | bytes 8388608

commit v3 on v2

--- a/solution.py
+++ b/solution.py
@@ -13,13 +13,19 @@
 NX, NY, NZ = 4, 8, 8
 COLOURS = 8
 ROWS = 128
+HALF = ROWS // 2
 
 decay_rate = 0.999
 rate_step = 0.125
 
-ALIKE = ((1, 1, -1), (-1, -1, 1), (-1, 2, 0), (1, -2, 0), (0, 3, -1), (0, -3, 1), (2, 4, 0))
+ALIKE = (
+    (1, 1, -1), (-1, -1, 1), (-1, 2, 0), (1, -2, 0), (1, 0, 2), (0, 3, -1), (0, -3, 1), (0, 1, -3), (0, -1, 3),
+    (0, 2, 2), (0, -2, -2), (1, 3, 1), (-1, -3, -1), (2, 4, 0), (1, 4, -2),
+)
 AROUND = ((1, 0, 0), (-1, 0, 0), (0, 1, 0), (0, -1, 0), (0, 0, 1), (0, 0, -1))
-ACROSS = ((0, 1, 1), (0, -1, -1)) + 6 * ((2, 0, 0),)
+UNITS = ((0, 0),) + tuple((dy, dx % 2) for dx, dy, dz in ALIKE)
+DETOUR = {(0, 1): (0, 1, 1), (1, 1): (0, -1, -1), (2, 1): (1, 0, -2), (2, 0): (-1, 0, 2), (-2, 1): (1, 0, -2), (-2, 0): (-1, 0, 2)}
+ACROSS = tuple(DETOUR.get(unit, (2, 0, 0)) for unit in UNITS)
 
 
 def pair_tables():
@@ -62,6 +68,8 @@
     z, x = lax.div(dp, NX), lax.rem(dp, NX)
     y, core = lax.div(fsdp, 2), lax.rem(fsdp, 2)
     colour = lax.rem(2 * x + y + 3 * z, COLOURS)
+    odd = lax.rem(x, 2)
+    parities = [odd, 1 - odd]
     xs = [lax.rem(x + d, NX) for d in range(NX)]
     ys = [lax.rem(y + d, NY) for d in range(NY)]
     zs = [lax.rem(z + d, NZ) for d in range(NZ)]
@@ -72,7 +80,7 @@
 
     twin = (dp, y * 2 + 1 - core)
 
-    own_rows = pl.ds(pl.multiple_of(colour * ROWS, ROWS), ROWS)
+    own_rows = pl.ds(pl.multiple_of(colour * ROWS + odd * HALF, HALF), HALF)
     loads = [
         pltpu.make_async_copy(source, target, loaded.at[number])
         for number, (source, target) in enumerate((
@@ -87,7 +95,7 @@
     barrier = pltpu.get_barrier_semaphore()
     for dx, dz in plane:
         pl.semaphore_signal(barrier, 1, device_id=chip(dx, 0, dz))
-    others = sorted(set(ALIKE + AROUND + ACROSS) - {(dx, 0, dz) for dx, dy, dz in AROUND if dy == 0} - {(2, 0, 0)})
+    others = sorted(step for step in set(ALIKE + AROUND + ACROSS) if step[1] != 0)
     for dx, dy, dz in others:
         pl.semaphore_signal(barrier, 1, device_id=chip(-dx, -dy, -dz))
     pl.semaphore_signal(barrier, 1, device_id=twin)
@@ -95,6 +103,7 @@
     lane = iota((8, 128), 1)
     even = iota((TOPK, 128), 1) % 2 == 0
     component = iota((STRETCH, 128), 0)
+    front = iota((TOPK, 128), 1) < HALF
 
     for load in loads[:4]:
         load.wait()
@@ -114,16 +123,28 @@
             jnp.where(even, listed[:TOPK], below[TOPK:]),
             jnp.where(even, above[:TOPK], listed[TOPK:]),
         )
+        picked = []
         for half in range(2):
             part = columns[STRETCH * half : STRETCH * (half + 1)]
             kept = jnp.zeros((STRETCH, 128), jnp.float32)
             for slot in range(TOPK):
                 match = component == places[half][slot : slot + 1]
-                picked = jnp.where(match, part, 0.0)
-                message[share, half, pl.ds(slot, 1), :] = jnp.sum(picked, axis=0, keepdims=True)
+                picked.append(jnp.sum(jnp.where(match, part, 0.0), axis=0, keepdims=True))
                 kept = jnp.where(match, part, kept)
             kept_columns[share, pl.ds(STRETCH * half, STRETCH), :] = kept
-        message[share, 2] = (places[0] + 65536 * places[1]).astype(jnp.float32)
+        for number, rows_of in enumerate((jnp.concatenate(picked, axis=0), jnp.concatenate(places, axis=0))):
+            turned = lane_gather(rows_of, (lane + HALF) % 128)
+            tiles = (
+                jnp.where(front, rows_of[:TOPK], turned[TOPK:]),
+                jnp.where(front, turned[:TOPK], rows_of[TOPK:]),
+            )
+            for half in range(2):
+                tile = tiles[half]
+                if number == 0:
+                    message[2 * share + half, 0] = tile[:2]
+                    message[2 * share + half, 1] = tile[2:]
+                else:
+                    message[2 * share + half, 2] = (tile[:2] + 65536 * tile[2:]).astype(jnp.float32)
         return carry
 
     lax.fori_loop(0, COLOURS, transform, 0)
@@ -132,7 +153,7 @@
 
     for number, (dx, dz) in enumerate(plane):
         pltpu.make_async_remote_copy(
-            src_ref=message.at[tints[(2 * dx + 3 * dz) % COLOURS]], dst_ref=inbox.at[number], send_sem=list_sent,
+            src_ref=message.at[2 * tints[(2 * dx + 3 * dz) % COLOURS] + parities[dx % 2]], dst_ref=inbox.at[number], send_sem=list_sent,
             recv_sem=list_here.at[number], device_id=chip(dx, 0, dz),
         ).start()
 
@@ -143,71 +164,78 @@
 
     lax.fori_loop(0, COLOURS, keep_rest, 0)
 
+    def list_sum(tile):
+        coded = tile[2].astype(jnp.int32)
+        places = (coded % 65536, coded // 65536)
+        term = jnp.zeros((STRETCH, 128), jnp.float32)
+        for slot in range(TOPK):
+            match = component == places[slot // 2][slot % 2 : slot % 2 + 1]
+            term = jnp.where(match, tile[slot // 2, pl.ds(slot % 2, 1), :], term)
+        return term
+
     def add_list(number, summed):
         pltpu.make_async_copy(inbox.at[number], inbox.at[number], list_here.at[number]).wait()
-        coded = inbox[number, 2].astype(jnp.int32)
-        places = (coded % 65536, coded // 65536)
-        halves = []
-        for half in range(2):
-            term = jnp.zeros((STRETCH, 128), jnp.float32)
-            for slot in range(TOPK):
-                match = component == places[half][slot : slot + 1]
-                term = jnp.where(match, inbox[number, half, pl.ds(slot, 1), :], term)
-            halves.append(summed[STRETCH * half : STRETCH * (half + 1)] + term)
-        return jnp.concatenate(halves, axis=0)
-
-    summed = lax.fori_loop(0, len(plane), add_list, kept_columns[colour])
-    restored = table_dot(summed.T, backward)
+        return summed + list_sum(inbox.at[number])
+
+    summed = lax.fori_loop(0, len(plane), add_list, list_sum(message.at[2 * colour + odd]))
+    turned = lane_gather(summed, (iota((STRETCH, 128), 1) + HALF) % 128)
+    restored = table_dot(jnp.concatenate([summed, turned], axis=0).T[:HALF], backward)
     loads[4].wait()
-    whole[y, core, colour] = (weight[...].astype(jnp.float32) - rate_step * restored).astype(jnp.bfloat16)
-
-    def block(plane, tint):
-        return whole.at[plane, core, tint]
-
-    def to_twin(plane, tint):
+    whole[y, core, colour, odd] = (weight[...].astype(jnp.float32) - rate_step * restored).astype(jnp.bfloat16)
+
+    def block(plane, tint, half):
+        return whole.at[plane, core, tint, half]
+
+    def send(what, sent, here, where):
         pltpu.make_async_remote_copy(
-            src_ref=block(plane, tint), dst_ref=block(plane, tint), send_sem=twin_sent,
-            recv_sem=twin_here, device_id=twin,
+            src_ref=what, dst_ref=what, send_sem=sent, recv_sem=here, device_id=where
         ).start()
 
-    def pass_on(plane, number):
+    def pass_on(number):
+        dy, parity = UNITS[number]
+        what = block(ys[-dy % NY], colour, parities[parity])
         for way, step in enumerate(AROUND + (ACROSS[number],)):
-            pltpu.make_async_remote_copy(
-                src_ref=block(plane, colour), dst_ref=block(plane, colour),
-                send_sem=around_sent, recv_sem=around_here.at[way, number], device_id=chip(*step),
-            ).start()
-        to_twin(plane, colour)
-
-    def await_block(plane, tint, semaphore):
-        pltpu.make_async_copy(block(plane, tint), block(plane, tint), semaphore).wait()
-
-    for number in reversed(range(len(ALIKE))):
-        pltpu.make_async_remote_copy(
-            src_ref=block(y, colour), dst_ref=block(y, colour), send_sem=alike_sent,
-            recv_sem=alike_here.at[number], device_id=chip(*ALIKE[number]),
-        ).start()
-    pass_on(y, 0)
+            send(what, around_sent, around_here.at[way, number], chip(*step))
+        send(what, twin_sent, twin_here, twin)
+
+    def collect(number):
+        dy, parity = UNITS[number]
+        for way, step in enumerate(AROUND + (ACROSS[number],)):
+            tint = tints[-(2 * step[0] + step[1] + 3 * step[2]) % COLOURS]
+            what = block(ys[(-step[1] - dy) % NY], tint, parities[(step[0] + parity) % 2])
+            pltpu.make_async_copy(what, what, around_here.at[way, number]).wait()
+            send(what, twin_sent, twin_here, twin)
+
     for number, step in enumerate(ALIKE):
-        there = ys[-step[1] % NY]
-        await_block(there, colour, alike_here.at[number])
-        pass_on(there, number + 1)
-
-    for number in range(NY):
-        back = 0 if number == 0 else ALIKE[number - 1][1]
-        for way, step in enumerate(AROUND + (ACROSS[number],)):
-            there = ys[(-step[1] - back) % NY]
-            tint = tints[-(2 * step[0] + step[1] + 3 * step[2]) % COLOURS]
-            await_block(there, tint, around_here.at[way, number])
-            to_twin(there, tint)
+        send(block(y, colour, odd), alike_sent.at[number // 14], alike_here.at[number], chip(*step))
+    pass_on(0)
+    for number, step in enumerate(ALIKE):
+        dy, parity = UNITS[number + 1]
+        what = block(ys[-dy % NY], colour, parities[parity])
+        pltpu.make_async_copy(what, what, alike_here.at[number]).wait()
+        pass_on(number + 1)
+    for number in range(len(UNITS)):
+        collect(number)
 
     def await_bytes(ref, semaphore):
         pltpu.make_async_copy(ref, ref, semaphore).wait()
 
     await_bytes(inbox, list_sent)
-    await_bytes(whole.at[pl.ds(0, 7), core, 0], alike_sent)
+    await_bytes(whole.at[0, core, pl.ds(0, 7)], alike_sent.at[0])
+    await_bytes(whole.at[0, core, 7, 0], alike_sent.at[1])
     await_bytes(whole.at[pl.ds(0, 7), core], around_sent)
     await_bytes(whole.at[:, core], twin_sent)
     await_bytes(whole.at[:, 1 - core], twin_here)
+
+
+def settle_kernel(moment_rows, whole, moment_out, weight_out, written):
+    copies = [pltpu.make_async_copy(moment_rows, moment_out, written.at[NY])]
+    for plane in range(NY):
+        copies.append(pltpu.make_async_copy(whole.at[plane], weight_out.at[plane], written.at[plane]))
+    for copy in copies:
+        copy.start()
+    for copy in copies:
+        copy.wait()
 
 
 def as_rows(array):
@@ -234,25 +262,36 @@
         sync_kernel,
         out_shape=(
             jax.ShapeDtypeStruct((rows, 128), jnp.float32),
-            jax.ShapeDtypeStruct((NY, 2, COLOURS, ROWS, 128), jnp.bfloat16),
+            jax.ShapeDtypeStruct((NY, 2, COLOURS, 2, HALF, 128), jnp.bfloat16),
         ),
         in_specs=[in_hbm] * 5,
         out_specs=(in_vmem, in_vmem),
         scratch_shapes=[
             pltpu.VMEM((rows, 128), jnp.float32),
             pltpu.VMEM((rows, 128), jnp.bfloat16),
-            pltpu.VMEM((ROWS, 128), jnp.bfloat16),
+            pltpu.VMEM((HALF, 128), jnp.bfloat16),
             pltpu.VMEM(indices.shape[1:], jnp.int32),
             pltpu.VMEM((2, 128, 128), jnp.float32),
             pltpu.VMEM((COLOURS, 128, ROWS), jnp.float32),
-            pltpu.VMEM((COLOURS, 3, TOPK, 128), jnp.float32),
-            pltpu.VMEM((peers, 3, TOPK, 128), jnp.float32),
-            dma((5,)), dma, dma((peers,)), dma, dma((len(ALIKE),)), dma, dma((7, NY)), dma, dma,
+            pltpu.VMEM((2 * COLOURS, 3, 2, 128), jnp.float32),
+            pltpu.VMEM((peers, 3, 2, 128), jnp.float32),
+            dma((5,)), dma, dma((peers,)), dma((2,)), dma((len(ALIKE),)), dma, dma((7, len(UNITS))), dma, dma,
         ],
         compiler_params=pltpu.CompilerParams(
             collective_id=0, has_side_effects=True, vmem_limit_bytes=24 * 2**20
         ),
     )(*(pltpu.with_memory_space_constraint(operand, pltpu.HBM) for operand in operands))
+    moment_rows, whole = pl.pallas_call(
+        settle_kernel,
+        out_shape=(
+            jax.ShapeDtypeStruct(moment_rows.shape, jnp.float32),
+            jax.ShapeDtypeStruct(whole.shape, jnp.bfloat16),
+        ),
+        in_specs=[in_vmem] * 2,
+        out_specs=(in_hbm, in_hbm),
+        scratch_shapes=[dma((NY + 1,))],
+        compiler_params=pltpu.CompilerParams(vmem_limit_bytes=8 * 2**20),
+    )(moment_rows, whole)
     weight_out = from_rows(whole.reshape(-1, 128), layers)
     return (from_rows(moment_rows, layers)[None], weight_out)
 

time: 49.6 us -> 45.2 us (0.911)
  local copies, waits for them, and re-layouts: 2.81 us -> 0 us
  Pallas kernels: 46 us -> 44.4 us
    pallas_call x1, Pallas kernels: 46 us -> 42.2 us  [shards(): pl.pallas_call(sync_kernel, out_shape=(jax.ShapeDtypeStruct((rows, 128),...]
    unnamed x2 -> x0, local copies, waits for them, and re-layouts: 2.81 us -> none
    pallas_call x0 -> x1, Pallas kernels: none -> 2.25 us  [shards(): pl.pallas_call(settle_kernel, out_shape=(jax.ShapeDtypeStruct(moment_rows...]
where the time goes in v3:
time: 45.2 us; the launch traced here: 45.1 us
  Pallas kernels  44.4 us (98%)
  between operations  0.64 us (1%)
    pallas_call x1, Pallas kernels, shards(): pl.pallas_call(sync_kernel, out_shape=(jax.ShapeDtypeStruct((rows, 128),...  42.2 us
    pallas_call x1, Pallas kernels, shards(): pl.pallas_call(settle_kernel, out_shape=(jax.ShapeDtypeStruct(moment_rows...  2.25 us

profile of v3, /device:TPU:1, one launch (start us, length us, event | category | flops | bytes accessed | tf_op | source)
XLA Modules:
  0.0 45.1 jit_solution(17856660559820888673)
XLA Ops:
  0.6 42.2 %shard_map.68 = (f32[1024,128]{1,0:T(8,128)S(1)}, bf16[8,2,8,2,64,128]{5,4,3,2,1,0:T(8,128)(2,1)S(1)}) custom-call(f32[1024,128]{1,0:T(8,128)} %bitcast.26, bf16[1024,128]{1,0:T(8,128)(2,1)} %bitcast.27, bf16[1024,128]{1,0:T(8,128)(2,1)} %bitcast.28, s32[2,4,1024]{2,1,0:T(4,128)} %bitcast.29, f32[2,128,128]{2,1,0:T(8,128)} %constant.2.clone.tables_in), custom_call_target="tpu_custom_call" | custom-call | tf_op jit(solution)/shard_map/pallas_call | solution.py:261
  42.8 2.3 %shard_map.69 = (f32[1024,128]{1,0:T(8,128)}, bf16[8,2,8,2,64,128]{5,4,3,2,1,0:T(8,128)(2,1)}) custom-call(f32[1024,128]{1,0:T(8,128)S(1)} %get-tuple-element.6.moment_rows, bf16[8,2,8,2,64,128]{5,4,3,2,1,0:T(8,128)(2,1)S(1)} %get-tuple-element.7.whole), custom_call_target="tpu_custom_call" | custom-call | tf_op jit(solution)/shard_map/pallas_call | solution.py:284

commit v4 on v3

--- a/solution.py
+++ b/solution.py
@@ -18,14 +18,45 @@
 decay_rate = 0.999
 rate_step = 0.125
 
-ALIKE = (
-    (1, 1, -1), (-1, -1, 1), (-1, 2, 0), (1, -2, 0), (1, 0, 2), (0, 3, -1), (0, -3, 1), (0, 1, -3), (0, -1, 3),
-    (0, 2, 2), (0, -2, -2), (1, 3, 1), (-1, -3, -1), (2, 4, 0), (1, 4, -2),
+STEPS = (
+    (0, -1, 0, 0), (0, 1, 0, 0), (0, 0, 0, -1), (0, -1, 1, 0), (0, 0, 0, 2), (0, 0, -2, 0), (0, 1, 0, -1),
+    (0, 0, 2, 0), (0, 0, 0, -2), (0, 0, 0, 1), (0, -1, -1, 0), (0, 0, -3, 1), (1, 0, 0, -1), (0, 2, 2, 0),
+    (2, 0, 0, 1), (3, 0, -1, 0), (4, 1, 0, 0), (4, 0, 0, 1), (0, -1, 4, 0), (0, -1, 0, -2), (6, 0, 0, -1),
+    (8, 0, 0, 1), (6, 1, 0, 0), (4, -1, 0, -1), (2, 1, 0, 0), (7, 1, 0, 0), (4, 0, 2, 0), (2, 0, 2, -1),
+    (8, 1, 0, 0), (11, -1, 0, 0), (4, -1, 0, 0), (5, 0, -3, 0), (11, 0, 0, 1), (9, 1, 0, 0), (6, 0, -1, -2),
+    (11, 0, 0, 2), (11, 0, -1, 0), (12, 0, 0, -1), (12, -1, 0, 0), (12, 0, 1, 0), (6, 1, -1, -1), (5, 0, 1, 0),
+    (4, 2, 0, 0), (16, -1, 0, 0), (16, 1, 0, 0), (14, 0, 0, 1), (6, 0, 1, 0), (15, 0, 1, 0), (15, 0, -1, 0),
+    (8, 0, 1, 0), (9, 0, -1, 0), (12, 1, -1, 0), (17, 0, 0, -1), (14, 0, 0, 2), (19, -1, 0, 0), (19, 0, 0, -1),
+    (12, 0, -2, 0), (18, 0, -1, 0), (19, 0, 0, 1), (8, 1, 1, -1), (21, 0, 0, -1), (26, 0, -1, 0), (13, 0, 1, 0),
+    (14, 0, 0, -1), (27, 0, 0, -1), (18, -1, 0, 0), (28, 0, 0, -1), (17, 0, 0, 1), (23, 0, 1, 0), (19, 1, 0, 0),
+    (21, -1, 0, 0), (22, -1, 0, 0), (23, 1, 0, 0), (27, 0, 0, 1), (27, -1, 0, 0), (27, 0, -1, 0), (30, 0, 0, 1),
+    (29, 0, 1, 0), (24, 1, 1, 0), (28, -1, 0, 0), (28, 0, -1, 0), (32, 0, 0, 1), (32, 1, 0, 0), (35, 0, 0, -1),
+    (24, 0, 2, 0), (33, 1, 0, 0), (34, 0, 1, 0), (32, 0, -1, 0), (41, -1, 0, 0), (39, 0, 0, 1), (36, 1, 0, 0),
+    (39, 0, 1, 0), (44, 0, 0, -1), (35, 0, -1, 0), (38, 1, 0, 0), (46, 0, 1, 0), (35, -1, 0, 1), (30, 0, -1, 1),
+    (36, 0, -1, 0), (46, -1, 0, 0), (40, 0, 0, 1), (52, 1, 0, 0), (52, 0, 0, -1), (52, 0, 1, 0), (37, 0, -1, 0),
+    (54, -1, 0, 0), (48, 0, 0, 1), (53, 0, 0, -1), (54, 0, 1, 0), (56, 1, 0, 0), (45, 0, -1, 0), (58, -1, 0, 0),
+    (52, 0, 0, 1), (55, 0, 0, -1), (55, 0, 1, 0), (57, 1, 0, 0), (49, 0, -1, 0), (61, -1, 0, 0), (57, 0, 0, 1),
+    (60, 0, 0, -1), (57, 0, 1, 0), (65, 1, 0, 0), (62, 0, -1, 0), (59, 0, 0, 1), (65, 0, 0, -1), (60, 0, 1, 0),
+    (67, 1, 0, 0),
 )
-AROUND = ((1, 0, 0), (-1, 0, 0), (0, 1, 0), (0, -1, 0), (0, 0, 1), (0, 0, -1))
-UNITS = ((0, 0),) + tuple((dy, dx % 2) for dx, dy, dz in ALIKE)
-DETOUR = {(0, 1): (0, 1, 1), (1, 1): (0, -1, -1), (2, 1): (1, 0, -2), (2, 0): (-1, 0, 2), (-2, 1): (1, 0, -2), (-2, 0): (-1, 0, 2)}
-ACROSS = tuple(DETOUR.get(unit, (2, 0, 0)) for unit in UNITS)
+SENDS = (
+    4, 6, 1, 8, 2, 5, 3, 7, 12, 9, 10, 19, 11, 20, 14, 13, 25, 28, 15, 16, 24, 31, 17, 27, 43, 18, 32, 42, 21, 47,
+    35, 23, 41, 26, 50, 22, 60, 29, 51, 34, 36, 30, 33, 37, 38, 40, 39, 52, 57, 63, 64, 54, 46, 48, 49, 44, 45, 53,
+    68, 66, 58, 55, 59, 56, 70, 61, 71, 72, 69, 73, 79, 85, 62, 65, 75, 74, 76, 67, 81, 80, 78, 98, 77, 82, 88, 83,
+    86, 87, 94, 97, 84, 91, 99, 105, 95, 90, 92, 101, 89, 93, 111, 100, 96, 107, 117, 113, 102, 103, 104, 108, 106,
+    109, 114, 115, 110, 119, 116, 121, 112, 124, 126, 120, 118, 123, 122, 125, 127,
+)
+
+
+def total_steps():
+    ways = [(0, 0, 0)]
+    for source, *jump in STEPS:
+        ways.append(tuple(a + b for a, b in zip(ways[source], jump)))
+    after = [[] for way in ways]
+    for number in SENDS:
+        source, *jump = STEPS[number - 1]
+        after[source].append((number, tuple(jump)))
+    return ways, after
 
 
 def pair_tables():
@@ -62,7 +93,7 @@
 
 def sync_kernel(momentum_in, gradients_in, weight_in, indices_in, tables_in, moment_out, whole,
                 momentum, gradients, weight, indices, tables, kept_columns, message, inbox, loaded,
-                list_sent, list_here, alike_sent, alike_here, around_sent, around_here, twin_sent, twin_here):
+                list_sent, list_here, passed_on, here, twin_sent, twin_here):
     dp = lax.axis_index("dp")
     fsdp = lax.axis_index("fsdp")
     z, x = lax.div(dp, NX), lax.rem(dp, NX)
@@ -91,11 +122,12 @@
     for load in loads:
         load.start()
 
-    plane = [(dx, dz) for dz in (4, 3, 5, 2, 6, 1, 7, 0) for dx in (2, 1, 3, 0) if (dx, dz) != (0, 0)]
+    plane = [(dx, dz) for dz in (0, 1, 7, 2, 6, 3, 5, 4) for dx in (0, 1, 3, 2) if (dx, dz) != (0, 0)]
     barrier = pltpu.get_barrier_semaphore()
-    for dx, dz in plane:
+    for dx, dz in reversed(plane):
         pl.semaphore_signal(barrier, 1, device_id=chip(dx, 0, dz))
-    others = sorted(step for step in set(ALIKE + AROUND + ACROSS) if step[1] != 0)
+    ways, after = total_steps()
+    others = sorted({(dx % NX, dy % NY, dz % NZ) for source, dx, dy, dz in STEPS if dy != 0})
     for dx, dy, dz in others:
         pl.semaphore_signal(barrier, 1, device_id=chip(-dx, -dy, -dz))
     pl.semaphore_signal(barrier, 1, device_id=twin)
@@ -147,11 +179,11 @@
                     message[2 * share + half, 2] = (tile[:2] + 65536 * tile[2:]).astype(jnp.float32)
         return carry
 
-    lax.fori_loop(0, COLOURS, transform, 0)
+    lax.fori_loop(0, COLOURS, transform, 0, unroll=4)
 
     pl.semaphore_wait(barrier, len(plane) + len(others) + 1)
 
-    for number, (dx, dz) in enumerate(plane):
+    for number, (dx, dz) in reversed(list(enumerate(plane))):
         pltpu.make_async_remote_copy(
             src_ref=message.at[2 * tints[(2 * dx + 3 * dz) % COLOURS] + parities[dx % 2]], dst_ref=inbox.at[number], send_sem=list_sent,
             recv_sem=list_here.at[number], device_id=chip(dx, 0, dz),
@@ -191,39 +223,27 @@
             src_ref=what, dst_ref=what, send_sem=sent, recv_sem=here, device_id=where
         ).start()
 
-    def pass_on(number):
-        dy, parity = UNITS[number]
-        what = block(ys[-dy % NY], colour, parities[parity])
-        for way, step in enumerate(AROUND + (ACROSS[number],)):
-            send(what, around_sent, around_here.at[way, number], chip(*step))
+    def have(number):
+        dx, dy, dz = ways[number]
+        what = block(ys[-dy % NY], tints[-(2 * dx + dy + 3 * dz) % COLOURS], parities[dx % 2])
+        if number > 0:
+            pltpu.make_async_copy(what, what, here.at[number]).wait()
+        for follower, step in after[number]:
+            send(what, passed_on.at[(sent[0] >= 112) + (sent[0] >= 126)], here.at[follower], chip(*step))
+            sent[0] += 1
         send(what, twin_sent, twin_here, twin)
 
-    def collect(number):
-        dy, parity = UNITS[number]
-        for way, step in enumerate(AROUND + (ACROSS[number],)):
-            tint = tints[-(2 * step[0] + step[1] + 3 * step[2]) % COLOURS]
-            what = block(ys[(-step[1] - dy) % NY], tint, parities[(step[0] + parity) % 2])
-            pltpu.make_async_copy(what, what, around_here.at[way, number]).wait()
-            send(what, twin_sent, twin_here, twin)
-
-    for number, step in enumerate(ALIKE):
-        send(block(y, colour, odd), alike_sent.at[number // 14], alike_here.at[number], chip(*step))
-    pass_on(0)
-    for number, step in enumerate(ALIKE):
-        dy, parity = UNITS[number + 1]
-        what = block(ys[-dy % NY], colour, parities[parity])
-        pltpu.make_async_copy(what, what, alike_here.at[number]).wait()
-        pass_on(number + 1)
-    for number in range(len(UNITS)):
-        collect(number)
+    sent = [0]
+    for number in range(len(ways)):
+        have(number)
 
     def await_bytes(ref, semaphore):
         pltpu.make_async_copy(ref, ref, semaphore).wait()
 
     await_bytes(inbox, list_sent)
-    await_bytes(whole.at[0, core, pl.ds(0, 7)], alike_sent.at[0])
-    await_bytes(whole.at[0, core, 7, 0], alike_sent.at[1])
-    await_bytes(whole.at[pl.ds(0, 7), core], around_sent)
+    await_bytes(whole.at[pl.ds(0, 7), core], passed_on.at[0])
+    await_bytes(whole.at[0, core, pl.ds(0, 7)], passed_on.at[1])
+    await_bytes(whole.at[0, core, 7, 0], passed_on.at[2])
     await_bytes(whole.at[:, core], twin_sent)
     await_bytes(whole.at[:, 1 - core], twin_here)
 
@@ -275,7 +295,7 @@
             pltpu.VMEM((COLOURS, 128, ROWS), jnp.float32),
             pltpu.VMEM((2 * COLOURS, 3, 2, 128), jnp.float32),
             pltpu.VMEM((peers, 3, 2, 128), jnp.float32),
-            dma((5,)), dma, dma((peers,)), dma((2,)), dma((len(ALIKE),)), dma, dma((7, len(UNITS))), dma, dma,
+            dma((5,)), dma, dma((peers,)), dma((3,)), dma((len(STEPS) + 1,)), dma, dma,
         ],
         compiler_params=pltpu.CompilerParams(
             collective_id=0, has_side_effects=True, vmem_limit_bytes=24 * 2**20

time: 45.2 us -> 44.2 us (0.978)
  Pallas kernels: 44.4 us -> 43.4 us
    pallas_call x1, Pallas kernels: 42.2 us -> 41.1 us  [shards(): pl.pallas_call(sync_kernel, out_shape=(jax.ShapeDtypeStruct((rows, 128),...]
where the time goes in v4:
time: 44.2 us; the launch traced here: 44 us
  Pallas kernels  43.4 us (98%)
  between operations  0.64 us (1%)
    pallas_call x1, Pallas kernels, shards(): pl.pallas_call(sync_kernel, out_shape=(jax.ShapeDtypeStruct((rows, 128),...  41.1 us
    pallas_call x1, Pallas kernels, shards(): pl.pallas_call(settle_kernel, out_shape=(jax.ShapeDtypeStruct(moment_rows...  2.25 us

profile of v4, /device:TPU:1, one launch (start us, length us, event | category | flops | bytes accessed | tf_op | source)
XLA Modules:
  0.0 44.0 jit_solution(6577016761300919714)
XLA Ops:
  0.6 41.1 %shard_map.68 = (f32[1024,128]{1,0:T(8,128)S(1)}, bf16[8,2,8,2,64,128]{5,4,3,2,1,0:T(8,128)(2,1)S(1)}) custom-call(f32[1024,128]{1,0:T(8,128)} %bitcast.26, bf16[1024,128]{1,0:T(8,128)(2,1)} %bitcast.27, bf16[1024,128]{1,0:T(8,128)(2,1)} %bitcast.28, s32[2,4,1024]{2,1,0:T(4,128)} %bitcast.29, f32[2,128,128]{2,1,0:T(8,128)} %constant.2.clone.tables_in), custom_call_target="tpu_custom_call" | custom-call | tf_op jit(solution)/shard_map/pallas_call | solution.py:281
  41.8 2.3 %shard_map.69 = (f32[1024,128]{1,0:T(8,128)}, bf16[8,2,8,2,64,128]{5,4,3,2,1,0:T(8,128)(2,1)}) custom-call(f32[1024,128]{1,0:T(8,128)S(1)} %get-tuple-element.6.moment_rows, bf16[8,2,8,2,64,128]{5,4,3,2,1,0:T(8,128)(2,1)S(1)} %get-tuple-element.7.whole), custom_call_target="tpu_custom_call" | custom-call | tf_op jit(solution)/shard_map/pallas_call | solution.py:304

commit v5 on v4

--- a/solution.py
+++ b/solution.py
@@ -124,12 +124,12 @@
 
     plane = [(dx, dz) for dz in (0, 1, 7, 2, 6, 3, 5, 4) for dx in (0, 1, 3, 2) if (dx, dz) != (0, 0)]
     barrier = pltpu.get_barrier_semaphore()
-    for dx, dz in reversed(plane):
-        pl.semaphore_signal(barrier, 1, device_id=chip(dx, 0, dz))
     ways, after = total_steps()
     others = sorted({(dx % NX, dy % NY, dz % NZ) for source, dx, dy, dz in STEPS if dy != 0})
-    for dx, dy, dz in others:
-        pl.semaphore_signal(barrier, 1, device_id=chip(-dx, -dy, -dz))
+    senders = [(-dx, -dy, -dz) for dx, dy, dz in others] + [(dx, 0, dz) for dx, dz in plane]
+    senders.sort(key=lambda step: -sum(min(d % n, -d % n) for d, n in zip(step, (NX, NY, NZ))))
+    for step in senders:
+        pl.semaphore_signal(barrier, 1, device_id=chip(*step))
     pl.semaphore_signal(barrier, 1, device_id=twin)
 
     lane = iota((8, 128), 1)

time: 44.2 us -> 43.6 us (0.986)
  Pallas kernels: 43.4 us -> 42.8 us
    pallas_call x1, Pallas kernels: 41.1 us -> 40.6 us  [shards(): pl.pallas_call(sync_kernel, out_shape=(jax.ShapeDtypeStruct((rows, 128),...]
where the time goes in v5:
time: 43.6 us; the launch traced here: 43.5 us
  Pallas kernels  42.8 us (98%)
  between operations  0.64 us (1%)
    pallas_call x1, Pallas kernels, shards(): pl.pallas_call(sync_kernel, out_shape=(jax.ShapeDtypeStruct((rows, 128),...  40.6 us
    pallas_call x1, Pallas kernels, shards(): pl.pallas_call(settle_kernel, out_shape=(jax.ShapeDtypeStruct(moment_rows...  2.25 us

profile of v5, /device:TPU:1, one launch (start us, length us, event | category | flops | bytes accessed | tf_op | source)
XLA Modules:
  0.0 43.5 jit_solution(12200939328751002576)
XLA Ops:
  0.6 40.6 %shard_map.68 = (f32[1024,128]{1,0:T(8,128)S(1)}, bf16[8,2,8,2,64,128]{5,4,3,2,1,0:T(8,128)(2,1)S(1)}) custom-call(f32[1024,128]{1,0:T(8,128)} %bitcast.26, bf16[1024,128]{1,0:T(8,128)(2,1)} %bitcast.27, bf16[1024,128]{1,0:T(8,128)(2,1)} %bitcast.28, s32[2,4,1024]{2,1,0:T(4,128)} %bitcast.29, f32[2,128,128]{2,1,0:T(8,128)} %constant.2.clone.tables_in), custom_call_target="tpu_custom_call" | custom-call | tf_op jit(solution)/shard_map/pallas_call | solution.py:281
  41.2 2.3 %shard_map.69 = (f32[1024,128]{1,0:T(8,128)}, bf16[8,2,8,2,64,128]{5,4,3,2,1,0:T(8,128)(2,1)}) custom-call(f32[1024,128]{1,0:T(8,128)S(1)} %get-tuple-element.6.moment_rows, bf16[8,2,8,2,64,128]{5,4,3,2,1,0:T(8,128)(2,1)S(1)} %get-tuple-element.7.whole), custom_call_target="tpu_custom_call" | custom-call | tf_op jit(solution)/shard_map/pallas_call | solution.py:304

commit v6 on v5

--- a/solution.py
+++ b/solution.py
@@ -112,11 +112,14 @@
     twin = (dp, y * 2 + 1 - core)
 
     own_rows = pl.ds(pl.multiple_of(colour * ROWS + odd * HALF, HALF), HALF)
+    first, second = pl.ds(0, COLOURS // 2 * ROWS), pl.ds(COLOURS // 2 * ROWS, COLOURS // 2 * ROWS)
     loads = [
         pltpu.make_async_copy(source, target, loaded.at[number])
         for number, (source, target) in enumerate((
-            (indices_in, indices), (tables_in, tables), (momentum_in, momentum),
-            (gradients_in, gradients), (weight_in.at[own_rows], weight),
+            (indices_in, indices), (tables_in, tables),
+            (momentum_in.at[first], momentum.at[first]), (gradients_in.at[first], gradients.at[first]),
+            (momentum_in.at[second], momentum.at[second]), (gradients_in.at[second], gradients.at[second]),
+            (weight_in.at[own_rows], weight),
         ))
     ]
     for load in loads:
@@ -179,7 +182,10 @@
                     message[2 * share + half, 2] = (tile[:2] + 65536 * tile[2:]).astype(jnp.float32)
         return carry
 
-    lax.fori_loop(0, COLOURS, transform, 0, unroll=4)
+    lax.fori_loop(0, COLOURS // 2, transform, 0, unroll=4)
+    for load in loads[4:6]:
+        load.wait()
+    lax.fori_loop(COLOURS // 2, COLOURS, transform, 0, unroll=4)
 
     pl.semaphore_wait(barrier, len(plane) + len(others) + 1)
 
@@ -212,7 +218,7 @@
     summed = lax.fori_loop(0, len(plane), add_list, list_sum(message.at[2 * colour + odd]))
     turned = lane_gather(summed, (iota((STRETCH, 128), 1) + HALF) % 128)
     restored = table_dot(jnp.concatenate([summed, turned], axis=0).T[:HALF], backward)
-    loads[4].wait()
+    loads[6].wait()
     whole[y, core, colour, odd] = (weight[...].astype(jnp.float32) - rate_step * restored).astype(jnp.bfloat16)
 
     def block(plane, tint, half):
@@ -295,7 +301,7 @@
             pltpu.VMEM((COLOURS, 128, ROWS), jnp.float32),
             pltpu.VMEM((2 * COLOURS, 3, 2, 128), jnp.float32),
             pltpu.VMEM((peers, 3, 2, 128), jnp.float32),
-            dma((5,)), dma, dma((peers,)), dma((3,)), dma((len(STEPS) + 1,)), dma, dma,
+            dma((7,)), dma, dma((peers,)), dma((3,)), dma((len(STEPS) + 1,)), dma, dma,
         ],
         compiler_params=pltpu.CompilerParams(
             collective_id=0, has_side_effects=True, vmem_limit_bytes=24 * 2**20

time: 43.6 us -> 43.6 us (level)
  no operation moved by 1% of the time
where the time goes in v6:
time: 43.6 us; the launch traced here: 43.5 us
  Pallas kernels  42.8 us (98%)
  between operations  0.64 us (1%)
    pallas_call x1, Pallas kernels, shards(): pl.pallas_call(sync_kernel, out_shape=(jax.ShapeDtypeStruct((rows, 128),...  40.6 us
    pallas_call x1, Pallas kernels, shards(): pl.pallas_call(settle_kernel, out_shape=(jax.ShapeDtypeStruct(moment_rows...  2.25 us

profile of v6, /device:TPU:1, one launch (start us, length us, event | category | flops | bytes accessed | tf_op | source)
XLA Modules:
  0.0 43.5 jit_solution(17910737126656039866)
XLA Ops:
  0.6 40.6 %shard_map.68 = (f32[1024,128]{1,0:T(8,128)S(1)}, bf16[8,2,8,2,64,128]{5,4,3,2,1,0:T(8,128)(2,1)S(1)}) custom-call(f32[1024,128]{1,0:T(8,128)} %bitcast.26, bf16[1024,128]{1,0:T(8,128)(2,1)} %bitcast.27, bf16[1024,128]{1,0:T(8,128)(2,1)} %bitcast.28, s32[2,4,1024]{2,1,0:T(4,128)} %bitcast.29, f32[2,128,128]{2,1,0:T(8,128)} %constant.2.clone.tables_in), custom_call_target="tpu_custom_call" | custom-call | tf_op jit(solution)/shard_map/pallas_call | solution.py:287
  41.2 2.3 %shard_map.69 = (f32[1024,128]{1,0:T(8,128)}, bf16[8,2,8,2,64,128]{5,4,3,2,1,0:T(8,128)(2,1)}) custom-call(f32[1024,128]{1,0:T(8,128)S(1)} %get-tuple-element.6.moment_rows, bf16[8,2,8,2,64,128]{5,4,3,2,1,0:T(8,128)(2,1)S(1)} %get-tuple-element.7.whole), custom_call_target="tpu_custom_call" | custom-call | tf_op jit(solution)/shard_map/pallas_call | solution.py:310
